TPU v7x, 512 devices: a whole 4x4x16 slice. The times are simulated.
512 devices in a mesh: depth: 16 (over x_hi, y, core), tile: 32 (over z, x_lo).
Axes of the slice: x: 4 (x_hi: 2, x_lo: 2; x = x_hi * 2 + x_lo), y: 4, z: 16, core: 2. Of those that a mesh axis runs over, the one named last changes fastest.
Arguments:
- volume: float32 [16, 1024, 1024], P('depth', 'tile'), may hold values from 0.05 to 100
- measured: float32 [1024, 1024], P('tile'), may hold values from 0.15 to 0.6
- point_spread: bfloat16 [16, 13, 13], P('depth'), may hold values from 7.390976e-05 to 0.0007362366
- entry_block: int32 [32, 4096], P('tile', 'depth'), may hold values from 0 to 63
- entry_neuron: int32 [32, 4096], P('tile', 'depth'), may hold values from -1 to 8191, as said below
- footprints: bfloat16 [32, 4096, 4, 128], P('tile', 'depth'), may hold values from 0.049804688 to 1
- seed_plane: int32 [8192], replicated, may hold values from 0 to 15
- seed_row: int32 [8192], replicated, may hold values from 0 to 1023
- seed_col: int32 [8192], replicated, may hold values from 0 to 1023
- owner_slot: int32 [8192], replicated, may hold values from 0 to 8191, each once
Outputs:
- estimate: float32 [16, 1024, 1024], P('depth', 'tile')
- demixed: float32 [8192], P(('depth', 'tile'))
Inputs may be any that keep to these rules, and one draw needn't show every extreme that they name: `entry_neuron`: -1 marks an empty slot; on each device the active slots come first, from 85 to 256 of them, and some device has all 256 slots active; neuron ids may repeat.
All inputs are finite; a program needn't handle non-finite values.
Results may differ from a plain program's by a relative error of at most 0.0025.
Values may be sent and summed in bfloat16 or wider, within the bound.
No kernel may reach another device: no remote copies, remote signals or barrier semaphores. Data moves between devices by JAX's collectives and lax.ppermute only.
A program may use at most 64 MiB of HBM per device.

v0:
```python
import jax
import jax.numpy as jnp
from jax import lax
from jax.sharding import PartitionSpec as P

ITERS = 2
RADIUS = 6
BR = 4
CB = 128


def padded_2(cells, sides, width):
    for axis, dim in sides:
        count = lax.axis_size(axis)
        ends = count - 1
        head = lax.slice_in_dim(cells, 0, width, axis=dim)
        tail = lax.slice_in_dim(cells, cells.shape[dim] - width, cells.shape[dim], axis=dim)
        cells = jnp.concatenate(
            [
                lax.ppermute(tail, axis, [(i, (i + 1) % count) for i in range(ends)]),
                cells,
                lax.ppermute(head, axis, [((i + 1) % count, i) for i in range(ends)]),
            ],
            axis=dim,
        )
    return cells


def band_tables(point_spread):
    kernel_size = point_spread.shape[1]
    radius = kernel_size // 2
    inner = jnp.arange(3 * CB)[:, None, None]
    outer = jnp.arange(CB)[None, :, None]
    tapnum = jnp.arange(kernel_size)[None, None, :]
    ahead_hot = (inner - CB - outer + radius == tapnum).astype(jnp.float32)
    behind_hot = (CB + outer + radius - inner == tapnum).astype(jnp.float32)
    spread_f = point_spread.astype(jnp.float32)
    high = lax.Precision.HIGHEST
    ahead = jnp.einsum("pak,jik->paji", spread_f, ahead_hot, precision=high).astype(jnp.bfloat16)
    behind = jnp.einsum("pak,jik->paji", spread_f, behind_hot, precision=high).astype(jnp.bfloat16)
    return (ahead, behind)


def column_blocks(field):
    shape = field.shape
    blocks = field.reshape(shape[:-1] + (shape[-1] // CB, CB))
    widths = [(0, 0)] * (len(shape) - 1)
    before = jnp.pad(blocks, widths + [(1, 0), (0, 0)])[..., :-1, :]
    after = jnp.pad(blocks, widths + [(0, 1), (0, 0)])[..., 1:, :]
    return jnp.concatenate([before, blocks, after], axis=-1)


def project_ahead(padded, ahead, rows_dev):
    stacked = column_blocks(padded)
    kernel_size = ahead.shape[1]
    summed = None
    for tapnum in range(kernel_size):
        term = jnp.einsum(
            "prnj,pji->rni",
            stacked[:, tapnum : tapnum + rows_dev],
            ahead[:, tapnum],
            preferred_element_type=jnp.float32,
        )
        summed = term if summed is None else summed + term
    return summed.reshape(rows_dev, -1)


def project_behind(padded, behind, rows_dev):
    stacked = column_blocks(padded)
    kernel_size = behind.shape[1]
    last = kernel_size - 1
    summed = None
    for tapnum in range(kernel_size):
        begin = last - tapnum
        term = jnp.einsum(
            "rnj,pji->prni",
            stacked[begin : begin + rows_dev],
            behind[:, tapnum],
            preferred_element_type=jnp.float32,
        )
        summed = term if summed is None else summed + term
    return summed.reshape(behind.shape[0], rows_dev, -1)


def body(
    volume,
    measured,
    point_spread,
    entry_block,
    entry_neuron,
    footprints,
    seed_plane,
    seed_row,
    seed_col,
    owner_slot,
):
    planes_dev, rows_dev, columns = volume.shape
    norm = jnp.sum(point_spread.astype(jnp.float32), axis=(1, 2))
    ahead, behind = band_tables(point_spread)
    estimate = volume
    for sweep in range(ITERS):
        rounded = estimate.astype(jnp.bfloat16)
        padded = padded_2(rounded, (("tile", 1),), RADIUS)
        partial_value = project_ahead(padded, ahead, rows_dev)
        plane_sum = lax.psum(partial_value.astype(jnp.bfloat16), "depth").astype(jnp.float32)
        ratio = (measured / plane_sum).astype(jnp.bfloat16)
        ratio_padded = padded_2(ratio, (("tile", 0),), RADIUS)
        backward = project_behind(ratio_padded, behind, rows_dev)
        estimate = estimate * backward / norm[:, None, None]
    row_groups = rows_dev // BR
    col_groups = columns // CB
    blocked = estimate.reshape(planes_dev, row_groups, BR, col_groups, CB).transpose(0, 1, 3, 2, 4)
    blocked = blocked.reshape(planes_dev * row_groups * col_groups, BR, CB)
    block_ids = entry_block[0]
    neuron = entry_neuron[0]
    weights = footprints[0].astype(jnp.float32)
    active = (neuron >= 0).astype(jnp.float32)
    neurons = seed_plane.shape[0]
    slot_pos = owner_slot[jnp.maximum(neuron, 0)]
    picked = blocked[block_ids]
    slot_proj = jnp.sum(weights * picked, axis=(1, 2)) * active
    proj_dense = jnp.zeros((neurons,), jnp.float32).at[slot_pos].add(slot_proj)
    holder = (seed_plane // planes_dev == lax.axis_index("depth")) & (
        seed_row // rows_dev == lax.axis_index("tile")
    )
    seed_value = estimate[seed_plane % planes_dev, seed_row % rows_dev, seed_col] * holder.astype(
        jnp.float32
    )
    seed_dense = jnp.zeros((neurons,), jnp.float32).at[owner_slot].add(seed_value)
    group = lax.axis_size(("depth", "tile"))
    owned_count = neurons // group
    proj_all, seed_all = lax.psum((proj_dense, seed_dense), ("depth", "tile"))
    offset = lax.axis_index(("depth", "tile")) * owned_count
    proj_own = lax.dynamic_slice_in_dim(proj_all, offset, owned_count, 0)
    seed_own = lax.dynamic_slice_in_dim(seed_all, offset, owned_count, 0)
    scaled = weights * (seed_all[slot_pos] * active)[:, None, None]
    block_count = blocked.shape[0]
    selector = (jnp.arange(block_count)[:, None] == block_ids[None, :]).astype(jnp.float32)
    rebuilt = jnp.dot(
        selector,
        scaled.reshape(scaled.shape[0], BR * CB),
        precision=lax.Precision.HIGHEST,
        preferred_element_type=jnp.float32,
    )
    rebuilt = rebuilt.reshape(block_count, BR, CB)
    slot_over = jnp.sum(weights * rebuilt[block_ids], axis=(1, 2)) * active
    over_dense = jnp.zeros((neurons,), jnp.float32).at[slot_pos].add(slot_over)
    over_own = lax.psum_scatter(over_dense, ("depth", "tile"), scatter_dimension=0, tiled=True)
    demixed = seed_own * proj_own / (over_own + 100.0 * seed_own)
    return (estimate, demixed)


def solution(mesh):
    in_specs = (
        P("depth", "tile", None),
        P("tile", None),
        P("depth", None, None),
        P("tile", "depth"),
        P("tile", "depth"),
        P("tile", "depth", None, None),
        P(),
        P(),
        P(),
        P(),
    )
    out_specs = (P("depth", "tile", None), P(("depth", "tile")))
    return jax.shard_map(body, mesh=mesh, in_specs=in_specs, out_specs=out_specs, check_vma=False)
```

profile of v0, /device:TPU:1, one launch (start us, length us, event | category | flops | bytes accessed | tf_op | source)
XLA Modules:
  0.0 1035.4 jit_solution(12849229935386808176)
XLA Ops:
  7.2 0.9 convert_element_type.84
  8.1 0.6 fusion.177
  8.7 4.5 collective-permute-start
  13.3 1.3 collective-permute-start.1
  14.7 1.6 fusion.7
  16.3 2.7 fusion.173
  19.1 0.9 fusion.6
  20.0 3.2 fusion.172
  23.3 1.7 gather_fusion.1
  25.1 0.8 pad_maximum_fusion.4
  28.8 0.2 fusion.10
  29.0 0.6 copy.297
  29.7 148.9 %all-reduce.14.cloned.1.call-done = bf16[32,1024]{1,0:T(8,128)(2,1)} async-done(((bf16[32,1024]{1,0:T(8,128)(2,1)}), bf16[32,1024]{1,0:T(8,128)(2,1)}) %all-reduce.14.cloned.1.call-update) | async-done | bytes 65552 | tf_op jit(solution)/shard_map/psum | solution.py:105
  178.6 0.9 divide_convert_fusion.1
  179.5 2.3 collective-permute-start.2
  181.9 1.3 collective-permute-start.3
  183.2 0.6 convert_reduce_fusion
  183.8 3.3 collective-permute-done.3
  187.3 1.2 fusion.41
  188.5 1.2 convolution_add_fusion.35
  189.7 0.2 convolution_add_fusion.34
  189.9 0.2 convolution_add_fusion.33
  190.9 0.2 convolution_add_fusion.29
  192.0 0.2 convolution_add_fusion.25
  192.2 0.2 fusion.9
  192.6 0.7 fusion.171
  193.3 4.4 collective-permute-start.4
  197.7 1.3 collective-permute-start.5
  199.0 3.2 collective-permute-done.5
  205.3 0.6 copy.296
  206.1 144.1 %all-reduce.16.cloned.1.call-done = bf16[32,1024]{1,0:T(8,128)(2,1)} async-done(((bf16[32,1024]{1,0:T(8,128)(2,1)}), bf16[32,1024]{1,0:T(8,128)(2,1)}) %all-reduce.16.cloned.1.call-update) | async-done | bytes 65552 | tf_op jit(solution)/shard_map/psum | solution.py:105
  350.2 0.9 divide_convert_fusion
  351.0 2.2 collective-permute-start.6
  353.2 1.5 collective-permute-start.7
  355.0 3.5 collective-permute-done.7
  361.8 0.7 fusion.44
  362.6 65.0 %gather_fusion = f32[8192]{0:T(1024)S(1)} fusion(f32[1,32,1024]{2,1,0:T(8,128)S(1)} %fusion.44, s32[8192]{0:T(1024)S(1)} %fusion.156), kind=kCustom, calls=%fused_computation | custom fusion | bytes 163840 | tf_op jit(solution)/shard_map/gather | solution.py:126
  427.6 43.2 %scatter_custom_fusion = f32[8192]{0:T(1024)S(1)} fusion(s32[8192]{0:T(1024)S(1)} %compare_select_fusion.2, f32[8192]{0:T(1024)S(1)} %and_select_fusion, f32[]{:T(128)} %constant.76.clone.1), kind=kCustom, calls=%fused_computation.290 | custom fusion | flops 8192 | bytes 32772 | tf_op jit(solution)/shard_map/scatter-add | solution.py:129
  470.9 109.2 %psum.30 = f32[8192]{0:T(1024)S(1)} all-reduce(f32[8192]{0:T(1024)S(1)} %scatter_custom_fusion), channel_id=1, replica_groups=mesh['depth'=16,'tile'=32] {'depth','tile'}, use_global_device_ids=true, to_apply=%region_4.5 | all-reduce | flops 8192 | bytes 65536 | tf_op jit(solution)/shard_map/psum | solution.py:132
  580.1 1.7 gather_fusion.3
  581.9 0.4 fusion.99
  582.6 1.0 gather_fusion.4
  583.6 1.0 gather_fusion.2
  584.6 1.0 fusion.12
  585.6 2.5 scatter_custom_fusion.1
  588.1 2.5 scatter_custom_fusion.2
  590.7 436.9 %all-reduce.18.cloned.1.call-done = (f32[8192]{0:T(1024)}, f32[8192]{0:T(1024)}) async-done(((f32[8192]{0:T(1024)}, f32[8192]{0:T(1024)}), (f32[8192]{0:T(1024)}, f32[8192]{0:T(1024)})) %all-reduce.18.cloned.1.call-update) | async-done | bytes 65552
  1027.6 1.3 fusion.170
  (165 shorter events, 11.6 us)
Async XLA Ops:
  7.2 171.5 %all-reduce.14.cloned.1.call-start = ((), (), s32[]{:S(2)}) async-start(), calls=%async_computation | async-start | bytes 131072 | tf_op jit(solution)/shard_map/psum | solution.py:105
  8.7 16.3 %collective-permute-start = (bf16[1,6,1024]{2,1,0:T(8,128)(2,1)}, bf16[1,6,1024]{2,1,0:T(8,128)(2,1)}, u32[]{:S(2)}, u32[]{:S(2)}) collective-permute-start(bf16[1,6,1024]{2,1,0:T(8,128)(2,1)} %get-tuple-element.46), channel_id=1, source_target_pairs={{0,1},{1,2},{2,3},{3,4},{4,5},{5,6},{6,7},{7,8},{8,9},{9,10},{10,1... | collective-permute-start | bytes 36872 | tf_op jit(solution)/shard_map/ppermute | solution.py:20
  13.3 11.8 %collective-permute-start.1 = (bf16[1,6,1024]{2,1,0:T(8,128)(2,1)}, bf16[1,6,1024]{2,1,0:T(8,128)(2,1)}, u32[]{:S(2)}, u32[]{:S(2)}) collective-permute-start(bf16[1,6,1024]{2,1,0:T(8,128)(2,1)} %get-tuple-element.47), channel_id=1, source_target_pairs={{1,0},{2,1},{3,2},{4,3},{5,4},{6,5},{7,6},{8,7},{9,8},{10,9},{11,1... | collective-permute-start | bytes 36872 | tf_op jit(solution)/shard_map/ppermute | solution.py:22
  16.3 2.7 copy-start.26
  19.0 7.5 copy-start.6
  19.0 7.7 copy-start.4
  20.0 3.3 copy-start.1
  20.0 3.2 copy-start.30
  20.0 5.0 copy-start.25
  20.0 5.0 copy-start.27
  27.8 1.9 copy-start.29
  27.9 150.8 %copy-start.8 = (f32[32,1024]{1,0:T(8,128)S(1)}, f32[32,1024]{1,0:T(8,128)}, u32[]{:S(2)}) copy-start(f32[32,1024]{1,0:T(8,128)} %param.11) | copy-start | bytes 393220
  29.7 320.5 %all-reduce.16.cloned.1.call-start = ((), (), s32[]{:S(2)}) async-start(), calls=%async_computation.1 | async-start | bytes 131072 | tf_op jit(solution)/shard_map/psum | solution.py:105
  179.5 10.2 copy-start.21
  179.5 4.2 collective-permute-start.2
  181.9 5.2 collective-permute-start.3
  187.2 3.1 copy-start.19
  188.5 2.2 copy-start.17
  189.9 1.0 copy-start.15
  190.4 1.0 copy-start.13
  190.4 1.2 copy-start.11
  190.6 1.2 copy-start.9
  191.3 1.3 copy-start.2
  192.5 10.3 copy-start.7
  193.3 9.8 copy-start.5
  193.3 5.7 collective-permute-start.4
  197.7 4.5 collective-permute-start.5
  204.2 150.6 %copy-start.3 = (bf16[1,256,4,128]{3,2,1,0:T(4,128)(2,1)S(1)}, bf16[1,256,4,128]{3,2,1,0:T(4,128)(2,1)}, u32[]{:S(2)}) copy-start(bf16[1,256,4,128]{3,2,1,0:T(4,128)(2,1)} %param.15) | copy-start | bytes 786436
  205.3 153.3 %copy-start.24 = (bf16[1,1,384,128]{3,1,2,0:T(2,128)(2,1)S(1)}, bf16[1,1,384,128]{3,1,2,0:T(2,128)(2,1)}, u32[]{:S(2)}) copy-start(bf16[1,1,384,128]{3,1,2,0:T(2,128)(2,1)} %get-tuple-element.18) | copy-start | bytes 294916
  206.0 821.6 %all-reduce.18.cloned.1.call-start = ((), (), s32[]{:S(2)}) async-start(), calls=%async_computation.2 | async-start | bytes 131072
  351.0 3.9 collective-permute-start.6
  353.2 5.2 collective-permute-start.7
  354.8 4.1 copy-start.23
  354.9 4.2 copy-start.22
  358.6 1.2 copy-start.20
  358.9 1.2 copy-start.18
  359.4 1.0 copy-start.16
  359.6 1.0 copy-start.14
  359.8 1.0 copy-start.12
  360.1 1.0 copy-start.10
  362.6 219.9 %copy-start = (f32[1,32,1024]{2,1,0:T(8,128)}, f32[1,32,1024]{2,1,0:T(8,128)S(1)}, u32[]{:S(2)}) copy-start(f32[1,32,1024]{2,1,0:T(8,128)S(1)} %fusion.44) | copy-start | bytes 393220
  362.6 65.0 %copy-start.28 = (s32[8192]{0:T(1024)S(1)}, s32[8192]{0:T(1024)}, u32[]{:S(2)}) copy-start(s32[8192]{0:T(1024)} %param.16) | copy-start | bytes 98308
Sparse Core Ops, SparseCore 0:
  29.8 148.7 all-reduce.13
  206.1 144.0 all-reduce.15
  590.8 436.7 all-reduce.17
where the time goes:
time: 1040 us
  waiting for transfers between devices  740 us (71%)
  blocking collectives  109 us (10%)
  local copies, waits for them, and re-layouts  79.5 us (8%)
  other arithmetic  56.6 us (5%)
  starting transfers between devices  18.9 us (2%)
  matrix products  16.2 us (2%)
  between operations  15.1 us (1%)
    unnamed x4, waiting for transfers between devices  437 us
    psum x2, waiting for transfers between devices, body(): lax.psum(partial_value.astype(jnp.bfloat16), 'depth').astype(jnp.float32)  293 us
    psum x1, blocking collectives, body(): proj_all, seed_all = lax.psum((proj_dense, seed_dense), ('depth', 'tile'))  109 us
    gather x1, local copies, waits for them, and re-layouts, body(): estimate[seed_plane % planes_dev, seed_row % rows_dev, seed_col]  65 us
    scatter-add x1, other arithmetic, body(): jnp.zeros((neurons,), jnp.float32).at[owner_slot].add(seed_value)  43.2 us
  transfers between devices with their start and end apart: 11, of which 6 were waited for; matrix products, arithmetic and copies ran while one was open for 1% of the time, Pallas kernels for 0%

commit v1 on v0

--- a/solution.py
+++ b/solution.py
@@ -129,7 +129,7 @@
     seed_dense = jnp.zeros((neurons,), jnp.float32).at[owner_slot].add(seed_value)
     group = lax.axis_size(("depth", "tile"))
     owned_count = neurons // group
-    proj_all, seed_all = lax.psum((proj_dense, seed_dense), ("depth", "tile"))
+    proj_all, seed_all = lax.psum(lax.psum((proj_dense, seed_dense), "depth"), "tile")
     offset = lax.axis_index(("depth", "tile")) * owned_count
     proj_own = lax.dynamic_slice_in_dim(proj_all, offset, owned_count, 0)
     seed_own = lax.dynamic_slice_in_dim(seed_all, offset, owned_count, 0)

time: 1040 us -> 964 us (0.927)
  waiting for transfers between devices: 740 us -> 304 us
  blocking collectives: 109 us -> 478 us
    unnamed x4 -> x2, waiting for transfers between devices: 437 us -> 0.03 us
    psum x1 -> x4, blocking collectives: 109 us -> 341 us  [the longest x2 185 us: body(): lax.psum(lax.psum((proj_dense, seed_dense), 'depth'), 'tile')]
    unnamed x0 -> x1, blocking collectives: none -> 137 us
  transfers between devices with their start and end apart: 11 -> 10, of which waited for: 6 -> 5; matrix products, arithmetic and copies ran while one was open for 1% -> 1% of each run, Pallas kernels for 0% -> 0%
where the time goes in v1:
time: 964 us
  blocking collectives  478 us (50%)
  waiting for transfers between devices  304 us (32%)
  local copies, waits for them, and re-layouts  79.5 us (8%)
  other arithmetic  54.8 us (6%)
  starting transfers between devices  18.3 us (2%)
  between operations  15.5 us (2%)
  matrix products  14.3 us (1%)
    psum x2, waiting for transfers between devices, body(): lax.psum(partial_value.astype(jnp.bfloat16), 'depth').astype(jnp.float32)  294 us
    psum x2, blocking collectives, body(): lax.psum(lax.psum((proj_dense, seed_dense), 'depth'), 'tile')  185 us
    psum x2, blocking collectives, body(): lax.psum((proj_dense, seed_dense), 'depth')  156 us
    unnamed x1, blocking collectives  137 us
    gather x1, local copies, waits for them, and re-layouts, body(): estimate[seed_plane % planes_dev, seed_row % rows_dev, seed_col]  65 us
    scatter-add x1, other arithmetic, body(): jnp.zeros((neurons,), jnp.float32).at[owner_slot].add(seed_value)  43.4 us
  transfers between devices with their start and end apart: 10, of which 5 were waited for; matrix products, arithmetic and copies ran while one was open for 1% of the time, Pallas kernels for 0%

profile of v1, /device:TPU:1, one launch (start us, length us, event | category | flops | bytes accessed | tf_op | source)
XLA Modules:
  0.0 963.6 jit_solution(1699311823204424648)
XLA Ops:
  7.2 0.9 convert_element_type.84
  8.1 0.6 fusion.177
  8.7 3.9 collective-permute-start
  12.7 1.3 collective-permute-start.1
  14.1 1.6 fusion.7
  15.7 2.7 fusion.173
  18.5 0.9 fusion.6
  19.4 3.2 fusion.172
  22.6 0.6 compare_select_fusion.2
  23.3 1.7 gather_fusion.1
  28.0 0.2 fusion.10
  28.3 0.6 copy.297
  29.0 149.5 %all-reduce.12.cloned.1.call-done = bf16[32,1024]{1,0:T(8,128)(2,1)} async-done(((bf16[32,1024]{1,0:T(8,128)(2,1)}), bf16[32,1024]{1,0:T(8,128)(2,1)}) %all-reduce.12.cloned.1.call-update) | async-done | bytes 65552 | tf_op jit(solution)/shard_map/psum | solution.py:105
  178.5 0.9 divide_convert_fusion.1
  179.4 2.3 collective-permute-start.2
  181.7 1.3 collective-permute-start.3
  183.0 0.6 convert_reduce_fusion
  183.6 3.3 collective-permute-done.3
  187.4 0.2 convolution_add_fusion.35
  187.8 0.2 convolution_add_fusion.33
  188.6 0.2 convolution_add_fusion.30
  190.0 0.2 convolution_add_fusion.25
  190.5 0.7 fusion.171
  191.2 4.4 collective-permute-start.4
  195.6 1.3 collective-permute-start.5
  197.0 3.1 collective-permute-done.5
  203.3 0.6 copy.296
  204.0 144.2 %all-reduce.14.cloned.1.call-done = bf16[32,1024]{1,0:T(8,128)(2,1)} async-done(((bf16[32,1024]{1,0:T(8,128)(2,1)}), bf16[32,1024]{1,0:T(8,128)(2,1)}) %all-reduce.14.cloned.1.call-update) | async-done | bytes 65552 | tf_op jit(solution)/shard_map/psum | solution.py:105
  348.1 0.9 divide_convert_fusion
  349.0 2.2 collective-permute-start.6
  351.2 1.5 collective-permute-start.7
  352.9 3.5 collective-permute-done.7
  359.8 0.7 fusion.44
  360.5 65.0 %gather_fusion = f32[8192]{0:T(1024)S(1)} fusion(f32[1,32,1024]{2,1,0:T(8,128)S(1)} %fusion.44, s32[8192]{0:T(1024)S(1)} %fusion.156), kind=kCustom, calls=%fused_computation | custom fusion | bytes 163840 | tf_op jit(solution)/shard_map/gather | solution.py:126
  425.6 43.4 %scatter_custom_fusion = f32[8192]{0:T(1024)S(1)} fusion(s32[8192]{0:T(1024)} %compare_select_fusion.2, f32[8192]{0:T(1024)S(1)} %and_select_fusion, f32[]{:T(128)} %constant.76.clone.1), kind=kCustom, calls=%fused_computation.290 | custom fusion | flops 8192 | bytes 33280 | tf_op jit(solution)/shard_map/scatter-add | solution.py:129
  469.0 63.3 %psum.44 = f32[8192]{0:T(1024)S(1)} all-reduce(f32[8192]{0:T(1024)S(1)} %scatter_custom_fusion), channel_id=1, replica_groups=mesh['depth'=16,'tile'=32] {'depth'}, use_global_device_ids=true, to_apply=%region_4.5 | all-reduce | flops 8192 | bytes 65536 | tf_op jit(solution)/shard_map/psum | solution.py:132
  532.3 93.9 %psum.45 = f32[8192]{0:T(1024)S(1)} all-reduce(f32[8192]{0:T(1024)S(1)} %psum.44), channel_id=1, replica_groups=mesh['depth'=16,'tile'=32] {'tile'}, use_global_device_ids=true, to_apply=%region_5.6 | all-reduce | flops 8192 | bytes 65536 | tf_op jit(solution)/shard_map/psum | solution.py:132
  626.1 1.7 gather_fusion.3
  627.9 0.4 fusion.99
  628.6 1.0 gather_fusion.4
  629.6 1.0 gather_fusion.2
  630.6 1.0 fusion.12
  631.6 2.0 scatter_custom_fusion.1
  633.6 92.7 %psum.46 = f32[8192]{0:T(1024)S(1)} all-reduce(f32[8192]{0:T(1024)S(1)} %scatter_custom_fusion.1), channel_id=1, replica_groups=mesh['depth'=16,'tile'=32] {'depth'}, use_global_device_ids=true, to_apply=%region_8.9 | all-reduce | flops 8192 | bytes 65536 | tf_op jit(solution)/shard_map/psum | solution.py:132
  726.3 90.8 %psum.47 = f32[8192]{0:T(1024)S(1)} all-reduce(f32[8192]{0:T(1024)S(1)} %psum.46), channel_id=1, replica_groups=mesh['depth'=16,'tile'=32] {'tile'}, use_global_device_ids=true, to_apply=%region_9.10 | all-reduce | flops 8192 | bytes 65536 | tf_op jit(solution)/shard_map/psum | solution.py:132
  817.1 2.0 scatter_custom_fusion.2
  819.1 137.1 %all-reduce.8 = f32[8192]{0:T(1024)S(1)} all-reduce(f32[8192]{0:T(1024)S(1)} %scatter_custom_fusion.2), channel_id=2, replica_groups=mesh['depth'=16,'tile'=32] {'depth','tile'}, use_global_device_ids=true, to_apply=%region_12.13.clone | all-reduce | flops 8192 | bytes 65536
  956.2 0.6 fusion.170
  (172 shorter events, 12.3 us)
Async XLA Ops:
  7.2 171.3 %all-reduce.12.cloned.1.call-start = ((), (), s32[]{:S(2)}) async-start(), calls=%async_computation | async-start | bytes 131072 | tf_op jit(solution)/shard_map/psum | solution.py:105
  8.7 16.3 %collective-permute-start = (bf16[1,6,1024]{2,1,0:T(8,128)(2,1)}, bf16[1,6,1024]{2,1,0:T(8,128)(2,1)S(1)}, u32[]{:S(2)}, u32[]{:S(2)}) collective-permute-start(bf16[1,6,1024]{2,1,0:T(8,128)(2,1)} %get-tuple-element.44), channel_id=1, source_target_pairs={{0,1},{1,2},{2,3},{3,4},{4,5},{5,6},{6,7},{7,8},{8,9},{9,10},{10,1... | collective-permute-start | bytes 36872 | tf_op jit(solution)/shard_map/ppermute | solution.py:20
  12.7 12.4 %collective-permute-start.1 = (bf16[1,6,1024]{2,1,0:T(8,128)(2,1)}, bf16[1,6,1024]{2,1,0:T(8,128)(2,1)S(1)}, u32[]{:S(2)}, u32[]{:S(2)}) collective-permute-start(bf16[1,6,1024]{2,1,0:T(8,128)(2,1)} %get-tuple-element.45), channel_id=1, source_target_pairs={{1,0},{2,1},{3,2},{4,3},{5,4},{6,5},{7,6},{8,7},{9,8},{10,9},{11,1... | collective-permute-start | bytes 36872 | tf_op jit(solution)/shard_map/ppermute | solution.py:22
  15.7 2.7 copy-start.28
  18.4 7.3 copy-start.6
  18.4 7.5 copy-start.4
  19.4 3.2 copy-start.1
  19.4 3.8 copy-start.32
  19.4 5.6 copy-start.27
  19.4 5.6 copy-start.29
  27.1 1.9 copy-start.31
  27.1 151.4 %copy-start.8 = (f32[32,1024]{1,0:T(8,128)S(1)}, f32[32,1024]{1,0:T(8,128)}, u32[]{:S(2)}) copy-start(f32[32,1024]{1,0:T(8,128)} %param.11) | copy-start | bytes 393220
  27.8 159.3 %copy-start.25 = (bf16[1,1,384,128]{3,1,2,0:T(2,128)(2,1)S(1)}, bf16[1,1,384,128]{3,1,2,0:T(2,128)(2,1)}, u32[]{:S(2)}) copy-start(bf16[1,1,384,128]{3,1,2,0:T(2,128)(2,1)} %get-tuple-element.16) | copy-start | bytes 294916
  28.3 159.1 %copy-start.23 = (bf16[1,1,384,128]{3,1,2,0:T(2,128)(2,1)S(1)}, bf16[1,1,384,128]{3,1,2,0:T(2,128)(2,1)}, u32[]{:S(2)}) copy-start(bf16[1,1,384,128]{3,1,2,0:T(2,128)(2,1)} %get-tuple-element.15) | copy-start | bytes 294916
  28.9 319.2 %all-reduce.14.cloned.1.call-start = ((), (), s32[]{:S(2)}) async-start(), calls=%async_computation.1 | async-start | bytes 131072 | tf_op jit(solution)/shard_map/psum | solution.py:105
  179.4 8.2 copy-start.21
  179.4 4.2 collective-permute-start.2
  181.7 5.2 collective-permute-start.3
  187.1 1.2 copy-start.19
  187.4 1.2 copy-start.17
  187.8 1.0 copy-start.15
  188.3 1.0 copy-start.13
  188.3 1.2 copy-start.11
  188.6 1.2 copy-start.9
  189.3 1.3 copy-start.2
  189.5 7.5 copy-start.33
  190.4 10.3 %copy-start.7 = (bf16[1,1,384,128]{3,1,2,0:T(2,128)(2,1)S(1)}, bf16[1,1,384,128]{3,1,2,0:T(2,128)(2,1)}, u32[]{:S(2)}) copy-start(bf16[1,1,384,128]{3,1,2,0:T(2,128)(2,1)} %copy-done.6) | copy-start | bytes 294916
  191.2 9.8 %copy-start.5 = (bf16[1,1,384,128]{3,1,2,0:T(2,128)(2,1)S(1)}, bf16[1,1,384,128]{3,1,2,0:T(2,128)(2,1)}, u32[]{:S(2)}) copy-start(bf16[1,1,384,128]{3,1,2,0:T(2,128)(2,1)} %copy-done.4) | copy-start | bytes 294916
  191.2 5.7 collective-permute-start.4
  195.6 4.5 collective-permute-start.5
  202.1 150.6 %copy-start.3 = (bf16[1,256,4,128]{3,2,1,0:T(4,128)(2,1)S(1)}, bf16[1,256,4,128]{3,2,1,0:T(4,128)(2,1)}, u32[]{:S(2)}) copy-start(bf16[1,256,4,128]{3,2,1,0:T(4,128)(2,1)} %param.15) | copy-start | bytes 786436
  203.3 153.3 %copy-start.26 = (bf16[1,1,384,128]{3,1,2,0:T(2,128)(2,1)S(1)}, bf16[1,1,384,128]{3,1,2,0:T(2,128)(2,1)}, u32[]{:S(2)}) copy-start(bf16[1,1,384,128]{3,1,2,0:T(2,128)(2,1)} %get-tuple-element.16) | copy-start | bytes 294916
  349.0 3.9 collective-permute-start.6
  351.2 5.2 collective-permute-start.7
  352.7 4.1 copy-start.24
  352.9 4.2 copy-start.22
  356.6 1.2 copy-start.20
  356.8 1.2 copy-start.18
  357.3 1.0 copy-start.16
  357.6 1.0 copy-start.14
  357.8 1.0 copy-start.12
  358.0 1.0 copy-start.10
  360.5 267.9 %copy-start = (f32[1,32,1024]{2,1,0:T(8,128)}, f32[1,32,1024]{2,1,0:T(8,128)S(1)}, u32[]{:S(2)}) copy-start(f32[1,32,1024]{2,1,0:T(8,128)S(1)} %fusion.44) | copy-start | bytes 393220
  360.5 65.0 %copy-start.30 = (s32[8192]{0:T(1024)S(1)}, s32[8192]{0:T(1024)}, u32[]{:S(2)}) copy-start(s32[8192]{0:T(1024)} %param.16) | copy-start | bytes 98308
Sparse Core Ops, SparseCore 0:
  29.1 149.3 all-reduce.11
  204.1 144.0 all-reduce.13
